TPU v7x, 32 devices: a whole 2x2x4 slice. The times are simulated.
32 devices in a mesh: parts: 2 (over x), ff: 16 (over z, y, core).
Axes of the slice: x: 2, y: 2, z: 4, core: 2. Of those that a mesh axis runs over, the one named last changes fastest.
Arguments:
- tokens: bfloat16 [512, 8192], P(('parts', 'ff')), parts along dimension 0, may hold values from -6 to 6
- gate_weight: bfloat16 [8192, 14784], P(None, 'ff'), may hold values from -0.0625 to 0.0625
- up_weight: bfloat16 [8192, 14784], P(None, 'ff'), may hold values from -0.0625 to 0.0625
- test_matrix: bfloat16 [14784, 256], P('ff'), may hold values from -0.046875 to 0.046875
Outputs:
- factor: float32 [14784, 512], P('ff', 'parts'), parts along dimension 1
There are 2 independent parts, one for each index of `parts`. A program takes and returns all parts, laid end to end along the dimension named above; an argument that names none is the same for every part. Nothing has to cross between parts.
All inputs are finite; a program needn't handle non-finite values.
Results may differ from a plain program's by a relative error of at most 0.015.
The roundings to bfloat16 on the way count: a program that leaves them out, or rounds other values in their place, can miss the bound.
Values may be sent and summed in bfloat16 or wider, within the bound.
A program may use at most 128 MiB of HBM per device.

v0:
```python
import jax
import jax.numpy as jnp
from jax import lax
from jax.sharding import PartitionSpec as P


def per_device(tokens, gate_weight, up_weight, test_matrix):
    tok_block = lax.all_gather(tokens, "ff", axis=0, tiled=True)
    gate_part = jnp.dot(tok_block, gate_weight, preferred_element_type=jnp.float32)
    up_part = jnp.dot(tok_block, up_weight, preferred_element_type=jnp.float32)
    key_rows = (jax.nn.silu(gate_part) * up_part).astype(jnp.bfloat16)
    partial_sketch = jnp.dot(key_rows, test_matrix, preferred_element_type=jnp.float32)
    sketch_rows = lax.psum(partial_sketch, "ff")
    core_matrix = jnp.dot(sketch_rows.T, sketch_rows, precision=lax.Precision.HIGHEST)
    sketch_low = sketch_rows.astype(jnp.bfloat16)
    sketch_y = jnp.dot(key_rows.T, sketch_low, preferred_element_type=jnp.float32)
    rank_width = core_matrix.shape[0]
    diag_shift = 0.1 * jnp.trace(core_matrix) / rank_width
    core_matrix = core_matrix + diag_shift * jnp.eye(rank_width, dtype=jnp.float32)
    chol_factor = jnp.linalg.cholesky(core_matrix)
    solved = jax.scipy.linalg.solve_triangular(chol_factor, sketch_y.T, lower=True)
    return solved.T


def solution(mesh):
    placed = (P(("parts", "ff"), None), P(None, "ff"), P(None, "ff"), P("ff", None))
    return jax.shard_map(
        per_device, mesh=mesh, in_specs=placed, out_specs=P("ff", "parts"), check_vma=False
    )
```

profile of v0, /device:TPU:1, one launch (start us, length us, event | category | flops | bytes accessed | tf_op | source)
XLA Modules:
  0.0 243.8 jit_solution(8581282451498644425)
XLA Ops:
  6.5 0.0 copy-start
  6.5 0.0 all-gather.2.cloned.1.call-start
  6.5 0.7 all-gather.2.cloned.1.call-update
  7.3 0.0 all-reduce.3.cloned.1.call-start
  7.3 55.3 %all-gather.2.cloned.1.call-done = bf16[256,8192]{1,0:T(8,128)(2,1)} async-done(((bf16[16,8192]{1,0:T(8,128)(2,1)}), bf16[256,8192]{1,0:T(8,128)(2,1)}) %all-gather.2.cloned.1.call-update) | async-done | bytes 4194320 | tf_op jit(solution)/shard_map/all_gather | solution.py:8
  62.6 10.8 %fusion.13 = f32[256,924]{0,1:T(8,128)S(1)} fusion(bf16[256,8192]{1,0:T(8,128)(2,1)} %all-gather.2.cloned.1.call-done, bf16[8192,924]{0,1:T(8,128)(2,1)} %param.5), kind=kOutput, calls=%fused_computation.37 | convolution fusion | flops 3875536896 | bytes 20279296 | tf_op jit(solution)/shard_map/dot_general | solution.py:9
  73.5 0.0 copy-done.1
  73.5 8.0 %fusion = bf16[256,924]{0,1:T(8,128)(2,1)S(1)} fusion(bf16[256,8192]{1,0:T(8,128)(2,1)S(1)} %copy-done.1, bf16[8192,924]{0,1:T(8,128)(2,1)} %param.6, f32[256,924]{0,1:T(8,128)S(1)} %fusion.13), kind=kOutput, calls=%fused_computation.3 | convolution fusion | flops 3876956160 | bytes 20752384 | tf_op jit(solution)/shard_map/dot_general | solution.py:10
  81.4 1.0 fusion.14
  82.5 0.0 all-reduce.3.cloned.1.call-update
  82.5 87.7 %all-reduce.3.cloned.1.call-done = f32[256,256]{1,0:T(8,128)} async-done(((f32[256,256]{1,0:T(8,128)}), f32[256,256]{1,0:T(8,128)}) %all-reduce.3.cloned.1.call-update) | async-done | bytes 262160 | tf_op jit(solution)/shard_map/psum | solution.py:13
  170.2 2.2 select_reduce_fusion
  172.5 0.1 copy.5
  173.3 0.1 fusion.4
  173.3 11.7 %cholesky.49 = f32[128,128]{1,0:T(8,128)S(1)} custom-call(f32[128,128]{1,0:T(8,128)S(1)} %cholesky.115), custom_call_target="Cholesky" | custom-call | tf_op jit(solution)/shard_map/jit(cholesky)/cholesky | solution.py:20
  185.1 9.8 %custom-call.15 = f32[1,128,128]{1,2,0:T(8,128)S(1)} custom-call(f32[1,128,128]{2,1,0:T(8,128)S(1)} %get-tuple-element.26), custom_call_target="InvertDiagBlocksLowerTriangular" | custom-call | tf_op jit(solution)/shard_map/jit(cholesky)/cholesky | solution.py:20
  194.9 0.2 constant_dynamic-update-slice_fusion.1
  195.1 0.3 convolution_subtract_fusion.1
  195.4 11.7 %cholesky.103 = f32[128,128]{1,0:T(8,128)S(1)} custom-call(f32[128,128]{1,0:T(8,128)S(1)} %convolution_subtract_fusion.1), custom_call_target="Cholesky" | custom-call | tf_op jit(solution)/shard_map/jit(cholesky)/cholesky | solution.py:20
  207.2 0.7 compare_reduce_fusion
  209.2 0.1 triangular_solve.65
  209.2 4.0 %while.1 = (s32[]{:T(128)}, f32[256,256]{1,0:T(8,128)S(1)}, s32[2,2]{1,0:T(2,128)S(1)}, f32[2,128,128]{2,1,0:T(8,128)S(1)}, s32[]{:T(128)}) while((s32[]{:T(128)}, f32[256,256]{1,0:T(8,128)S(1)}, s32[2,2]{1,0:T(2,128)S(1)}, f32[2,128,128]{2,1,0:T(8,128)S(1)}, s32[]{:T(128)}) %tuple.24), condition=%wide.while_cond, body=%wide.while_body.sunk | while | flops 2 | bytes 131181 | solution.py:21
  209.2 0.6 fusion.29
  209.8 1.4 bitcast_dynamic-update-slice_fusion.2
  211.2 0.6 fusion.29
  211.8 1.4 bitcast_dynamic-update-slice_fusion.2
  213.2 19.9 %custom-call.16 = f32[2,128,128]{1,2,0:T(8,128)S(1)} custom-call(f32[2,128,128]{2,1,0:T(8,128)S(1)} %get-tuple-element.12), custom_call_target="InvertDiagBlocksLowerTriangular" | custom-call | tf_op jit(solution)/shard_map/jit(_solve_triangular)/triangular_solve | solution.py:21
  233.1 1.2 fusion.5
  234.3 0.5 fusion.1
  234.9 0.5 convolution_subtract_fusion
  235.4 0.5 fusion.8
  236.0 1.0 maximum_bitcast_fusion
  (11 shorter events, 0.2 us)
Async XLA Ops:
  6.5 74.9 %copy-start = (bf16[924,256]{1,0:T(8,128)(2,1)S(1)}, bf16[924,256]{1,0:T(8,128)(2,1)}, u32[]{:S(2)}) copy-start(bf16[924,256]{1,0:T(8,128)(2,1)} %param.7) | copy-start | bytes 1419268
  6.5 56.1 %all-gather.2.cloned.1.call-start = ((), (), s32[]{:S(2)}) async-start(), calls=%async_computation | async-start | bytes 4456448 | tf_op jit(solution)/shard_map/all_gather | solution.py:8
  7.3 163.0 %all-reduce.3.cloned.1.call-start = ((), (), s32[]{:S(2)}) async-start(), calls=%async_computation.1 | async-start | bytes 524288 | tf_op jit(solution)/shard_map/psum | solution.py:13
  62.6 10.8 %copy-start.1 = (bf16[256,8192]{1,0:T(8,128)(2,1)S(1)}, bf16[256,8192]{1,0:T(8,128)(2,1)}, u32[]{:S(2)}) copy-start(bf16[256,8192]{1,0:T(8,128)(2,1)} %all-gather.2.cloned.1.call-done) | copy-start | bytes 12582916
Sparse Core Ops, SparseCore 0:
  9.5 53.0 all-gather.1
  82.6 87.5 all-reduce.2
where the time goes:
time: 244 us
  waiting for transfers between devices  144 us (59%)
  other arithmetic  55 us (23%)
  matrix products  25.4 us (10%)
  between operations  15.5 us (6%)
  local copies, waits for them, and re-layouts  4.16 us (2%)
    psum x1, waiting for transfers between devices, per_device(): sketch_rows = lax.psum(partial_sketch, 'ff')  87.7 us
    all_gather x1, waiting for transfers between devices, per_device(): tok_block = lax.all_gather(tokens, 'ff', axis=0, tiled=True)  55.3 us
    another operation x6, other arithmetic, per_device(): chol_factor = jnp.linalg.cholesky(core_matrix)  34 us
    another operation x3, other arithmetic, per_device(): jax.scipy.linalg.solve_triangular(chol_factor, sketch_y.T, lower=True)  19.9 us
    dot_general x1, matrix products, per_device(): jnp.dot(tok_block, gate_weight, preferred_element_type=jnp.float32)  10.8 us
    dot_general x1, matrix products, per_device(): up_part = jnp.dot(tok_block, up_weight, preferred_element_type=jnp.float32)  7.96 us
  transfers between devices with their start and end apart: 2, of which 2 were waited for; matrix products, arithmetic and copies ran while one was open for 0% of the time, Pallas kernels for 0%

commit v1 on v0

v1 whole, which is shorter than its diff:
```python
import functools

import jax
import jax.numpy as jnp
from jax import lax
from jax.experimental import pallas as pl
from jax.experimental.pallas import tpu as pltpu
from jax.sharding import PartitionSpec as P

MESH = pl.DeviceIdType.MESH
CHUNKS = 4


def keys_kernel(n, tok_hbm, gate_hbm, up_hbm, test_ref, key_ref, sketch_ref,
                tok, gw, uw, gacc, uacc, part, sib_sum, half_sum, slices, full,
                loc_sem, w_sem, xs, xr, zs, zr, ys, yr, ss, sr,
                r0s, r0r, r1s, r1r, r2s, r2r, r3s, r3r):
    t, width = tok_hbm.shape
    kc = width // (2 * CHUNKS)
    chips, lines = n // 2, n // 4
    rows = n * t
    me = lax.axis_index("ff")
    core, chip = me % 2, me // 2
    b, a = chip % 2, chip // 2
    sibling = chip * 2 + (1 - core)

    def same_core(other_chip):
        return other_chip * 2 + core

    def line_chip(step, side):
        return ((a - step + lines) % lines) * 2 + side

    def send(src, dst, ssem, rsem, target):
        return pltpu.make_async_remote_copy(
            src_ref=src, dst_ref=dst, send_sem=ssem, recv_sem=rsem,
            device_id={"ff": target}, device_id_type=MESH)

    def own_copy(g):
        return pltpu.make_async_copy(
            tok_hbm.at[:, pl.ds(g * kc, kc)], tok.at[g, pl.ds(me * t, t), :], loc_sem.at[g])

    def gate_copy(g):
        return pltpu.make_async_copy(gate_hbm.at[pl.ds(g * kc, kc), :], gw.at[g], w_sem.at[0, g])

    def up_copy(g):
        return pltpu.make_async_copy(up_hbm.at[pl.ds(g * kc, kc), :], uw.at[g], w_sem.at[1, g])

    for i in range(CHUNKS):
        own_copy((1 - core) * CHUNKS + i).start()
    for i in range(CHUNKS):
        own_copy(core * CHUNKS + i).start()
    for i in range(CHUNKS):
        for h in (core, 1 - core):
            gate_copy(h * CHUNKS + i).start()
            up_copy(h * CHUNKS + i).start()

    barrier = pltpu.get_barrier_semaphore()
    pl.semaphore_signal(barrier, inc=1, device_id={"ff": sibling}, device_id_type=MESH)
    for d in range(1, chips):
        pl.semaphore_signal(barrier, inc=1, device_id={"ff": same_core((chip + d) % chips)}, device_id_type=MESH)
    pl.semaphore_wait(barrier, chips)

    def chip_rows(c):
        return pl.ds(pl.multiple_of(c * 2 * t, 2 * t), 2 * t)

    def pair_copy(g):
        own = tok.at[g, pl.ds(me * t, t), :]
        return send(own, own, xs.at[g], xr.at[g], sibling)

    def z_copy(i, d):
        block = tok.at[core * CHUNKS + i, chip_rows(chip), :]
        return send(block, block, zs.at[i, d], zr.at[i, d], same_core(((a + d) % lines) * 2 + b))

    def y_copy(i, d):
        block = tok.at[core * CHUNKS + i, chip_rows(line_chip(d, b)), :]
        return send(block, block, ys.at[i, d], yr.at[i, d], same_core(a * 2 + (1 - b)))

    def pass_copy(i, d, other):
        side = 1 - b if other else b
        block = tok.at[core * CHUNKS + i, chip_rows(line_chip(d, side)), :]
        return send(block, block, ss.at[i, other, d], sr.at[i, other, d], sibling)

    for i in range(CHUNKS):
        g = (1 - core) * CHUNKS + i
        own_copy(g).wait()
        pair_copy(g).start()
    for i in range(CHUNKS):
        g = core * CHUNKS + i
        own_copy(g).wait()
        pair_copy(g).start()
    for i in range(CHUNKS):
        pair_copy(core * CHUNKS + i).wait_recv()
        for d in range(1, lines):
            z_copy(i, d).start()
        y_copy(i, 0).start()

    gacc[...] = jnp.zeros_like(gacc)
    uacc[...] = jnp.zeros_like(uacc)

    def multiply(g):
        gate_copy(g).wait()
        up_copy(g).wait()
        gacc[...] += jnp.dot(tok[g], gw[g], preferred_element_type=jnp.float32)
        uacc[...] += jnp.dot(tok[g], uw[g], preferred_element_type=jnp.float32)

    def chunk(i, carry):
        for d in range(1, lines):
            z_copy(i, d).wait_recv()
            y_copy(i, d).start()
            pass_copy(i, d, 0).start()
        for d in range(lines):
            y_copy(i, d).wait_recv()
            pass_copy(i, d, 1).start()

        def halves(k, carry):
            h = (core + k) % 2

            @pl.when(k == 1)
            def _():
                pair_copy((1 - core) * CHUNKS + i).wait_recv()
                for d in range(lines):
                    if d > 0:
                        pass_copy(i, d, 0).wait_recv()
                    pass_copy(i, d, 1).wait_recv()

            multiply(h * CHUNKS + i)
            return carry

        return lax.fori_loop(0, 2, halves, carry)

    lax.fori_loop(0, CHUNKS, chunk, 0)

    gate = gacc[...]
    keys = (gate / (1.0 + jnp.exp(-gate)) * uacc[...]).astype(jnp.bfloat16)
    key_ref[...] = keys
    part[...] = jnp.dot(keys, test_ref[...], preferred_element_type=jnp.float32)

    half = rows // 2
    pair = send(part.at[pl.ds((1 - core) * half, half), :], sib_sum, r0s, r0r, sibling)
    pair.start()
    pair.wait_recv()
    half_sum[...] = part[pl.ds(core * half, half), :] + sib_sum[...]

    def slice_copy(d):
        target = (chip + d) % chips
        return send(half_sum.at[pl.ds(target * t, t), :], slices.at[d], r1s.at[d], r1r.at[d], same_core(target))

    for d in range(1, chips):
        slice_copy(d).start()
    total = half_sum[pl.ds(chip * t, t), :]
    for d in range(1, chips):
        slice_copy(d).wait_recv()
        total = total + slices[d]
    full[pl.ds(core * half + chip * t, t), :] = total

    def back_copy(d):
        own = full.at[pl.ds(core * half + chip * t, t), :]
        return send(own, own, r2s.at[d], r2r.at[d], same_core((chip + d) % chips))

    def back_pass(d):
        block = full.at[pl.ds(core * half + ((chip - d + chips) % chips) * t, t), :]
        return send(block, block, r3s.at[d], r3r.at[d], sibling)

    for d in range(1, chips):
        back_copy(d).start()
    back_pass(0).start()
    for d in range(1, chips):
        back_copy(d).wait_recv()
        back_pass(d).start()
    for d in range(chips):
        back_pass(d).wait_recv()
    sketch_ref[...] = full[...]

    def drain(i, carry):
        pair_copy(i).wait_send()
        pair_copy(CHUNKS + i).wait_send()
        for d in range(lines):
            if d > 0:
                z_copy(i, d).wait_send()
                pass_copy(i, d, 0).wait_send()
            y_copy(i, d).wait_send()
            pass_copy(i, d, 1).wait_send()
        return carry

    lax.fori_loop(0, CHUNKS, drain, 0)
    pair.wait_send()
    for d in range(1, chips):
        slice_copy(d).wait_send()
        back_copy(d).wait_send()
    for d in range(chips):
        back_pass(d).wait_send()


def keys_and_sketch(n, tokens, gate_weight, up_weight, test_matrix):
    t, width = tokens.shape
    hidden = gate_weight.shape[1]
    rank = test_matrix.shape[1]
    rows, kc = n * t, width // (2 * CHUNKS)
    chips, lines = n // 2, n // 4
    vmem, dma = pltpu.VMEM, pltpu.SemaphoreType.DMA
    f32, bf16 = jnp.float32, jnp.bfloat16
    return pl.pallas_call(
        functools.partial(keys_kernel, n),
        out_shape=(jax.ShapeDtypeStruct((rows, hidden), bf16), jax.ShapeDtypeStruct((rows, rank), f32)),
        in_specs=[pl.BlockSpec(memory_space=pl.ANY)] * 3 + [pl.BlockSpec(memory_space=pltpu.VMEM)],
        out_specs=(pl.BlockSpec(memory_space=pltpu.VMEM),) * 2,
        scratch_shapes=[
            vmem((2 * CHUNKS, rows, kc), bf16),
            vmem((2 * CHUNKS, kc, hidden), bf16),
            vmem((2 * CHUNKS, kc, hidden), bf16),
            vmem((rows, hidden), f32),
            vmem((rows, hidden), f32),
            vmem((rows, rank), f32),
            vmem((rows // 2, rank), f32),
            vmem((rows // 2, rank), f32),
            vmem((chips, t, rank), f32),
            vmem((rows, rank), f32),
            dma((2 * CHUNKS,)),
            dma((2, 2 * CHUNKS)),
            dma((2 * CHUNKS,)), dma((2 * CHUNKS,)),
            dma((CHUNKS, lines)), dma((CHUNKS, lines)),
            dma((CHUNKS, lines)), dma((CHUNKS, lines)),
            dma((CHUNKS, 2, lines)), dma((CHUNKS, 2, lines)),
            dma, dma,
            dma((chips,)), dma((chips,)),
            dma((chips,)), dma((chips,)),
            dma((chips,)), dma((chips,)),
        ],
        compiler_params=pltpu.CompilerParams(
            collective_id=0, has_side_effects=True, vmem_limit_bytes=56 * 2**20),
    )(tokens, gate_weight, up_weight, test_matrix)


def solution(mesh):
    n = mesh.shape["ff"]

    def per_device(tokens, gate_weight, up_weight, test_matrix):
        key_rows, sketch_rows = keys_and_sketch(n, tokens, gate_weight, up_weight, test_matrix)
        core_matrix = jnp.dot(sketch_rows.T, sketch_rows, precision=lax.Precision.HIGHEST)
        sketch_low = sketch_rows.astype(jnp.bfloat16)
        sketch_y = jnp.dot(key_rows.T, sketch_low, preferred_element_type=jnp.float32)
        rank_width = core_matrix.shape[0]
        diag_shift = 0.1 * jnp.trace(core_matrix) / rank_width
        core_matrix = core_matrix + diag_shift * jnp.eye(rank_width, dtype=jnp.float32)
        chol_factor = jnp.linalg.cholesky(core_matrix)
        solved = jax.scipy.linalg.solve_triangular(chol_factor, sketch_y.T, lower=True)
        return solved.T

    placed = (P(("parts", "ff"), None), P(None, "ff"), P(None, "ff"), P("ff", None))
    return jax.shard_map(
        per_device, mesh=mesh, in_specs=placed, out_specs=P("ff", "parts"), check_vma=False
    )
```

time: 244 us -> 184 us (0.75)
  waiting for transfers between devices: 144 us -> 0 us
  Pallas kernels: 0 us -> 71.4 us
  local copies, waits for them, and re-layouts: 4.16 us -> 48.1 us
  matrix products: 25.4 us -> 5.76 us
  between operations: 15.5 us -> 2.12 us
    psum x1 -> x0, waiting for transfers between devices: 87.7 us -> none  [per_device(): sketch_rows = lax.psum(partial_sketch, 'ff')]
    pallas_call x0 -> x1, Pallas kernels: none -> 71.4 us  [keys_and_sketch(): pl.pallas_call(functools.partial(keys_kernel, n), out_shape=(jax.ShapeDty...]
    all_gather x1 -> x0, waiting for transfers between devices: 55.3 us -> none  [per_device(): tok_block = lax.all_gather(tokens, 'ff', axis=0, tiled=True)]
    unnamed x4 -> x2, local copies, waits for them, and re-layouts: 0.01 us -> 43.9 us
    dot_general x3 -> x0, matrix products: 19.8 us -> none  [the longest x1 10.8 us: per_device(): jnp.dot(tok_block, gate_weight, preferred_element_type=jnp.float32)]
  transfers between devices with their start and end apart: 2 -> 0, of which waited for: 2 -> 0; matrix products, arithmetic and copies ran while one was open for 0% -> 0% of each run, Pallas kernels for 0% -> 0%
where the time goes in v1:
time: 184 us; the launch traced here: 182 us
  Pallas kernels  71.4 us (39%)
  other arithmetic  55 us (30%)
  local copies, waits for them, and re-layouts  48.1 us (26%)
  matrix products  5.76 us (3%)
  between operations  2.12 us (1%)
    pallas_call x1, Pallas kernels, keys_and_sketch(): pl.pallas_call(functools.partial(keys_kernel, n), out_shape=(jax.ShapeDty...  71.4 us
    unnamed x2, local copies, waits for them, and re-layouts  43.9 us
    another operation x6, other arithmetic, per_device(): chol_factor = jnp.linalg.cholesky(core_matrix)  34 us
    another operation x3, other arithmetic, per_device(): jax.scipy.linalg.solve_triangular(chol_factor, sketch_y.T, lower=True)  19.9 us
    another operation x6, local copies, waits for them, and re-layouts  4.02 us

profile of v1, /device:TPU:1, one launch (start us, length us, event | category | flops | bytes accessed | tf_op | source)
XLA Modules:
  0.0 182.4 jit_solution(182443983440593750)
XLA Ops:
  0.0 21.9 %copy.5.gate_hbm = bf16[8192,924]{1,0:T(8,128)(2,1)} copy(bf16[8192,924]{0,1:T(8,128)(2,1)} %param.5) | data formatting | bytes 30277632 | tf_op args[1]
  21.9 21.9 %copy.6.up_hbm = bf16[8192,924]{1,0:T(8,128)(2,1)} copy(bf16[8192,924]{0,1:T(8,128)(2,1)} %param.6) | data formatting | bytes 30277632 | tf_op args[2]
  43.9 71.4 %shard_map.46 = (bf16[256,924]{1,0:T(8,128)(2,1)}, f32[256,256]{1,0:T(8,128)}) custom-call(bf16[16,8192]{1,0:T(8,128)(2,1)} %tok_hbm.1, bf16[8192,924]{1,0:T(8,128)(2,1)} %copy.5.gate_hbm, bf16[8192,924]{1,0:T(8,128)(2,1)} %copy.6.up_hbm, bf16[924,256]{1,0:T(8,128)(2,1)} %test_ref.1), custom_call_target="tpu_custom_call" | custom-call | tf_op jit(solution)/shard_map/pallas_call | solution.py:202
  115.3 2.2 %select_reduce_fusion = (f32[]{:T(128)}, f32[256,256]{1,0:T(8,128)S(1)}) fusion(f32[256,256]{1,0:T(8,128)} %get-tuple-element.7), kind=kOutput, calls=%fused_computation.12 | convolution fusion | flops 201523200 | bytes 524292 | tf_op jit(solution)/shard_map/dot_general | solution.py:239
  117.5 0.1 copy.7
  118.3 0.1 fusion.3
  118.4 11.7 %cholesky.49 = f32[128,128]{1,0:T(8,128)S(1)} custom-call(f32[128,128]{1,0:T(8,128)S(1)} %cholesky.115), custom_call_target="Cholesky" | custom-call | tf_op jit(solution)/shard_map/jit(cholesky)/cholesky | solution.py:245
  130.1 9.8 %custom-call.15 = f32[1,128,128]{1,2,0:T(8,128)S(1)} custom-call(f32[1,128,128]{2,1,0:T(8,128)S(1)} %get-tuple-element.30), custom_call_target="InvertDiagBlocksLowerTriangular" | custom-call | tf_op jit(solution)/shard_map/jit(cholesky)/cholesky | solution.py:245
  140.0 0.2 constant_dynamic-update-slice_fusion.1
  140.2 0.3 convolution_subtract_fusion.1
  140.4 11.7 %cholesky.103 = f32[128,128]{1,0:T(8,128)S(1)} custom-call(f32[128,128]{1,0:T(8,128)S(1)} %convolution_subtract_fusion.1), custom_call_target="Cholesky" | custom-call | tf_op jit(solution)/shard_map/jit(cholesky)/cholesky | solution.py:245
  152.2 0.7 compare_reduce_fusion
  154.3 0.1 triangular_solve.65
  154.4 4.1 %while.1 = (s32[]{:T(128)}, f32[256,256]{1,0:T(8,128)S(1)}, s32[2,2]{1,0:T(2,128)S(1)}, f32[2,128,128]{2,1,0:T(8,128)S(1)}, s32[]{:T(128)}) while((s32[]{:T(128)}, f32[256,256]{1,0:T(8,128)S(1)}, s32[2,2]{1,0:T(2,128)S(1)}, f32[2,128,128]{2,1,0:T(8,128)S(1)}, s32[]{:T(128)}) %tuple.24), condition=%wide.while_cond, body=%wide.while_body.sunk | while | flops 2 | bytes 131181 | solution.py:246
  154.4 0.7 fusion.20
  155.1 1.3 bitcast_dynamic-update-slice_fusion.2
  156.4 0.7 fusion.20
  157.1 1.3 bitcast_dynamic-update-slice_fusion.2
  158.4 19.9 %custom-call.16 = f32[2,128,128]{1,2,0:T(8,128)S(1)} custom-call(f32[2,128,128]{2,1,0:T(8,128)S(1)} %get-tuple-element.16), custom_call_target="InvertDiagBlocksLowerTriangular" | custom-call | tf_op jit(solution)/shard_map/jit(_solve_triangular)/triangular_solve | solution.py:246
  178.3 1.5 fusion.4
  179.8 0.5 fusion
  180.3 0.5 convolution_subtract_fusion
  180.9 0.5 fusion.7
  181.4 1.0 maximum_bitcast_fusion
  (9 shorter events, 0.1 us)

commit v2 on v1

--- a/solution.py
+++ b/solution.py
@@ -9,6 +9,11 @@
 
 MESH = pl.DeviceIdType.MESH
 CHUNKS = 4
+
+
+def contract(x, y, x_dim, y_dim, precision=None):
+    return lax.dot_general(x, y, (((x_dim,), (y_dim,)), ((), ())), precision=precision,
+                           preferred_element_type=jnp.float32)
 
 
 def keys_kernel(n, tok_hbm, gate_hbm, up_hbm, test_ref, key_ref, sketch_ref,
@@ -40,10 +45,10 @@
             tok_hbm.at[:, pl.ds(g * kc, kc)], tok.at[g, pl.ds(me * t, t), :], loc_sem.at[g])
 
     def gate_copy(g):
-        return pltpu.make_async_copy(gate_hbm.at[pl.ds(g * kc, kc), :], gw.at[g], w_sem.at[0, g])
+        return pltpu.make_async_copy(gate_hbm.at[:, pl.ds(g * kc, kc)], gw.at[g], w_sem.at[0, g])
 
     def up_copy(g):
-        return pltpu.make_async_copy(up_hbm.at[pl.ds(g * kc, kc), :], uw.at[g], w_sem.at[1, g])
+        return pltpu.make_async_copy(up_hbm.at[:, pl.ds(g * kc, kc)], uw.at[g], w_sem.at[1, g])
 
     for i in range(CHUNKS):
         own_copy((1 - core) * CHUNKS + i).start()
@@ -100,8 +105,9 @@
     def multiply(g):
         gate_copy(g).wait()
         up_copy(g).wait()
-        gacc[...] += jnp.dot(tok[g], gw[g], preferred_element_type=jnp.float32)
-        uacc[...] += jnp.dot(tok[g], uw[g], preferred_element_type=jnp.float32)
+        block = tok[g]
+        gacc[...] += contract(gw[g], block, 1, 1)
+        uacc[...] += contract(uw[g], block, 1, 1)
 
     def chunk(i, carry):
         for d in range(1, lines):
@@ -133,7 +139,7 @@
     gate = gacc[...]
     keys = (gate / (1.0 + jnp.exp(-gate)) * uacc[...]).astype(jnp.bfloat16)
     key_ref[...] = keys
-    part[...] = jnp.dot(keys, test_ref[...], preferred_element_type=jnp.float32)
+    part[...] = contract(keys, test_ref[...], 0, 0)
 
     half = rows // 2
     pair = send(part.at[pl.ds((1 - core) * half, half), :], sib_sum, r0s, r0r, sibling)
@@ -193,7 +199,7 @@
 
 def keys_and_sketch(n, tokens, gate_weight, up_weight, test_matrix):
     t, width = tokens.shape
-    hidden = gate_weight.shape[1]
+    hidden = gate_weight.shape[0]
     rank = test_matrix.shape[1]
     rows, kc = n * t, width // (2 * CHUNKS)
     chips, lines = n // 2, n // 4
@@ -201,15 +207,15 @@
     f32, bf16 = jnp.float32, jnp.bfloat16
     return pl.pallas_call(
         functools.partial(keys_kernel, n),
-        out_shape=(jax.ShapeDtypeStruct((rows, hidden), bf16), jax.ShapeDtypeStruct((rows, rank), f32)),
+        out_shape=(jax.ShapeDtypeStruct((hidden, rows), bf16), jax.ShapeDtypeStruct((rows, rank), f32)),
         in_specs=[pl.BlockSpec(memory_space=pl.ANY)] * 3 + [pl.BlockSpec(memory_space=pltpu.VMEM)],
         out_specs=(pl.BlockSpec(memory_space=pltpu.VMEM),) * 2,
         scratch_shapes=[
             vmem((2 * CHUNKS, rows, kc), bf16),
-            vmem((2 * CHUNKS, kc, hidden), bf16),
-            vmem((2 * CHUNKS, kc, hidden), bf16),
-            vmem((rows, hidden), f32),
-            vmem((rows, hidden), f32),
+            vmem((2 * CHUNKS, hidden, kc), bf16),
+            vmem((2 * CHUNKS, hidden, kc), bf16),
+            vmem((hidden, rows), f32),
+            vmem((hidden, rows), f32),
             vmem((rows, rank), f32),
             vmem((rows // 2, rank), f32),
             vmem((rows // 2, rank), f32),
@@ -235,10 +241,10 @@
     n = mesh.shape["ff"]
 
     def per_device(tokens, gate_weight, up_weight, test_matrix):
-        key_rows, sketch_rows = keys_and_sketch(n, tokens, gate_weight, up_weight, test_matrix)
+        key_rows, sketch_rows = keys_and_sketch(n, tokens, gate_weight.T, up_weight.T, test_matrix)
         core_matrix = jnp.dot(sketch_rows.T, sketch_rows, precision=lax.Precision.HIGHEST)
         sketch_low = sketch_rows.astype(jnp.bfloat16)
-        sketch_y = jnp.dot(key_rows.T, sketch_low, preferred_element_type=jnp.float32)
+        sketch_y = jnp.dot(key_rows, sketch_low, preferred_element_type=jnp.float32)
         rank_width = core_matrix.shape[0]
         diag_shift = 0.1 * jnp.trace(core_matrix) / rank_width
         core_matrix = core_matrix + diag_shift * jnp.eye(rank_width, dtype=jnp.float32)

time: 184 us -> 138 us (0.75)
  local copies, waits for them, and re-layouts: 48.1 us -> 4.25 us
    unnamed x2 -> x0, local copies, waits for them, and re-layouts: 43.9 us -> none
where the time goes in v2:
time: 138 us; the launch traced here: 137 us
  Pallas kernels  70.3 us (51%)
  other arithmetic  55 us (40%)
  matrix products  5.72 us (4%)
  local copies, waits for them, and re-layouts  4.25 us (3%)
  between operations  1.99 us (1%)
    pallas_call x1, Pallas kernels, keys_and_sketch(): pl.pallas_call(functools.partial(keys_kernel, n), out_shape=(jax.ShapeDty...  70.3 us
    another operation x6, other arithmetic, per_device(): chol_factor = jnp.linalg.cholesky(core_matrix)  34 us
    another operation x3, other arithmetic, per_device(): jax.scipy.linalg.solve_triangular(chol_factor, sketch_y.T, lower=True)  19.9 us
    another operation x6, local copies, waits for them, and re-layouts  4.02 us

profile of v2, /device:TPU:1, one launch (start us, length us, event | category | flops | bytes accessed | tf_op | source)
XLA Modules:
  0.0 137.3 jit_solution(2756654546422876343)
XLA Ops:
  0.0 0.1 triangular_solve.65
  0.1 70.3 %shard_map.46 = (bf16[924,256]{1,0:T(8,128)(2,1)}, f32[256,256]{1,0:T(8,128)}) custom-call(bf16[16,8192]{1,0:T(8,128)(2,1)} %tok_hbm.1, bf16[924,8192]{1,0:T(8,128)(2,1)} %bitcast.40, bf16[924,8192]{1,0:T(8,128)(2,1)} %bitcast.41, bf16[924,256]{1,0:T(8,128)(2,1)} %test_ref.1), custom_call_target="tpu_custom_call" | custom-call | tf_op jit(solution)/shard_map/pallas_call | solution.py:208
  70.4 2.2 %select_reduce_fusion = (f32[]{:T(128)}, f32[256,256]{1,0:T(8,128)S(1)}) fusion(f32[256,256]{1,0:T(8,128)} %get-tuple-element.7), kind=kOutput, calls=%fused_computation.12 | convolution fusion | flops 201523200 | bytes 524292 | tf_op jit(solution)/shard_map/dot_general | solution.py:245
  73.3 1.4 %fusion.4 = f32[256,924]{0,1:T(8,128)S(1)} fusion(bf16[924,256]{1,0:T(8,128)(2,1)} %get-tuple-element.8, f32[256,256]{1,0:T(8,128)} %get-tuple-element.7), kind=kOutput, calls=%fused_computation.15 | convolution fusion | flops 121176064 | bytes 1681408 | tf_op jit(solution)/shard_map/dot_general | solution.py:247
  74.7 0.1 copy.5
  74.8 0.1 fusion.3
  74.9 11.7 %cholesky.49 = f32[128,128]{1,0:T(8,128)S(1)} custom-call(f32[128,128]{1,0:T(8,128)S(1)} %cholesky.115), custom_call_target="Cholesky" | custom-call | tf_op jit(solution)/shard_map/jit(cholesky)/cholesky | solution.py:251
  86.7 9.8 %custom-call.15 = f32[1,128,128]{1,2,0:T(8,128)S(1)} custom-call(f32[1,128,128]{2,1,0:T(8,128)S(1)} %get-tuple-element.30), custom_call_target="InvertDiagBlocksLowerTriangular" | custom-call | tf_op jit(solution)/shard_map/jit(cholesky)/cholesky | solution.py:251
  96.5 0.2 constant_dynamic-update-slice_fusion.1
  96.7 0.3 convolution_subtract_fusion.1
  97.0 11.7 %cholesky.103 = f32[128,128]{1,0:T(8,128)S(1)} custom-call(f32[128,128]{1,0:T(8,128)S(1)} %convolution_subtract_fusion.1), custom_call_target="Cholesky" | custom-call | tf_op jit(solution)/shard_map/jit(cholesky)/cholesky | solution.py:251
  108.7 0.7 compare_reduce_fusion
  110.7 4.1 %while.1 = (s32[]{:T(128)}, f32[256,256]{1,0:T(8,128)S(1)}, s32[2,2]{1,0:T(2,128)S(1)}, f32[2,128,128]{2,1,0:T(8,128)S(1)}, s32[]{:T(128)}) while((s32[]{:T(128)}, f32[256,256]{1,0:T(8,128)S(1)}, s32[2,2]{1,0:T(2,128)S(1)}, f32[2,128,128]{2,1,0:T(8,128)S(1)}, s32[]{:T(128)}) %tuple.24), condition=%wide.while_cond, body=%wide.while_body.sunk | while | flops 2 | bytes 131189 | solution.py:252
  110.8 0.7 fusion.20
  111.4 1.3 bitcast_dynamic-update-slice_fusion.2
  112.8 0.7 fusion.20
  113.5 1.3 bitcast_dynamic-update-slice_fusion.2
  114.8 19.9 %custom-call.16 = f32[2,128,128]{1,2,0:T(8,128)S(1)} custom-call(f32[2,128,128]{2,1,0:T(8,128)S(1)} %get-tuple-element.16), custom_call_target="InvertDiagBlocksLowerTriangular" | custom-call | tf_op jit(solution)/shard_map/jit(_solve_triangular)/triangular_solve | solution.py:252
  134.7 0.5 fusion
  135.2 0.6 convolution_subtract_fusion
  135.8 0.5 fusion.7
  136.3 1.0 maximum_bitcast_fusion
  (9 shorter events, 0.1 us)

commit v3 on v2

--- a/solution.py
+++ b/solution.py
@@ -237,20 +237,84 @@
     )(tokens, gate_weight, up_weight, test_matrix)
 
 
+def factor_kernel(key_ref, sketch_ref, out_ref, work):
+    rank = out_ref.shape[1]
+    span = work.shape[1]
+    tile, step = 128, 8
+    sketch = sketch_ref[...]
+    core_matrix = contract(sketch, sketch, 0, 0, lax.Precision.HIGHEST)
+    diag = (lax.broadcasted_iota(jnp.int32, (rank, rank), 0)
+            == lax.broadcasted_iota(jnp.int32, (rank, rank), 1))
+    shift = 0.1 * jnp.sum(jnp.where(diag, core_matrix, 0.0)) / rank
+    work[:, :rank] = core_matrix + jnp.where(diag, shift, 0.0)
+    work[:, rank:] = sketch.astype(jnp.bfloat16).astype(jnp.float32).T
+    row_id = lax.broadcasted_iota(jnp.int32, (step, tile), 0)
+
+    for k in range(0, rank, step):
+        first = k // tile * tile
+        head = work[k:k + step, first:first + tile]
+        a = [[jnp.broadcast_to(head[i:i + 1, k - first + j:k - first + j + 1], (step, tile))
+              for j in range(i + 1)] for i in range(step)]
+        low = [[None] * step for _ in range(step)]
+        inv = [[None] * step for _ in range(step)]
+        for j in range(step):
+            inv[j][j] = lax.rsqrt(a[j][j])
+            for i in range(j + 1, step):
+                low[i][j] = a[i][j] * inv[j][j]
+            for i in range(j + 1, step):
+                for m in range(j + 1, i + 1):
+                    a[i][m] = a[i][m] - low[i][j] * low[m][j]
+        for j in range(step):
+            for i in range(j + 1, step):
+                total = low[i][j] * inv[j][j]
+                for m in range(j + 1, i):
+                    total = total + low[i][m] * inv[m][j]
+                inv[i][j] = -inv[i][i] * total
+        columns = []
+        for j in range(step):
+            column = jnp.zeros((step, tile), jnp.float32)
+            for i in range(j, step):
+                column = jnp.where(row_id == i, inv[i][j], column)
+            columns.append(column)
+        tiles = []
+        for c in range(first, span, tile):
+            block = head if c == first else work[k:k + step, c:c + tile]
+            total = columns[0] * block[0:1, :]
+            for j in range(1, step):
+                total = total + columns[j] * block[j:j + 1, :]
+            if c >= rank:
+                work[k:k + step, c:c + tile] = total
+            tiles.append(total)
+        if k + step < rank:
+            solved = jnp.concatenate(tiles, axis=1)
+            turned = solved[:, :rank - first].T[k + step - first:, :]
+            work[k + step:, first:] -= contract(turned, solved, 1, 0, lax.Precision.HIGHEST)
+    basis = work[:, rank:]
+    high = basis.astype(jnp.bfloat16)
+    rest = (basis - high.astype(jnp.float32)).astype(jnp.bfloat16)
+    keys = key_ref[...]
+    out_ref[...] = contract(keys, high, 1, 1) + contract(keys, rest, 1, 1)
+
+
+def factor_of(key_rows, sketch_rows):
+    hidden, rows = key_rows.shape
+    rank = sketch_rows.shape[1]
+    return pl.pallas_call(
+        factor_kernel,
+        out_shape=jax.ShapeDtypeStruct((hidden, rank), jnp.float32),
+        in_specs=[pl.BlockSpec(memory_space=pltpu.VMEM)] * 2,
+        out_specs=pl.BlockSpec(memory_space=pltpu.VMEM),
+        scratch_shapes=[pltpu.VMEM((rank, rank + rows), jnp.float32)],
+        compiler_params=pltpu.CompilerParams(vmem_limit_bytes=32 * 2**20),
+    )(key_rows, sketch_rows)
+
+
 def solution(mesh):
     n = mesh.shape["ff"]
 
     def per_device(tokens, gate_weight, up_weight, test_matrix):
         key_rows, sketch_rows = keys_and_sketch(n, tokens, gate_weight.T, up_weight.T, test_matrix)
-        core_matrix = jnp.dot(sketch_rows.T, sketch_rows, precision=lax.Precision.HIGHEST)
-        sketch_low = sketch_rows.astype(jnp.bfloat16)
-        sketch_y = jnp.dot(key_rows, sketch_low, preferred_element_type=jnp.float32)
-        rank_width = core_matrix.shape[0]
-        diag_shift = 0.1 * jnp.trace(core_matrix) / rank_width
-        core_matrix = core_matrix + diag_shift * jnp.eye(rank_width, dtype=jnp.float32)
-        chol_factor = jnp.linalg.cholesky(core_matrix)
-        solved = jax.scipy.linalg.solve_triangular(chol_factor, sketch_y.T, lower=True)
-        return solved.T
+        return factor_of(key_rows, sketch_rows)
 
     placed = (P(("parts", "ff"), None), P(None, "ff"), P(None, "ff"), P("ff", None))
     return jax.shard_map(

time: 138 us -> 92.8 us (0.67)
  other arithmetic: 55 us -> 0 us
  Pallas kernels: 70.3 us -> 90.6 us
  matrix products: 5.72 us -> 0 us
  local copies, waits for them, and re-layouts: 4.25 us -> 1.97 us
  between operations: 1.99 us -> 0.02 us
    another operation x9 -> x0, other arithmetic: 53.9 us -> none  [the longest x6 34 us: per_device(): chol_factor = jnp.linalg.cholesky(core_matrix)]
    pallas_call x0 -> x1, Pallas kernels: none -> 20.3 us  [factor_of(): pl.pallas_call(factor_kernel, out_shape=jax.ShapeDtypeStruct((hidden, ran...]
    another operation x9 -> x0, local copies, waits for them, and re-layouts: 4.12 us -> none
    dot_general x2 -> x0, matrix products: 3.63 us -> none  [the longest x1 2.24 us: per_device(): jnp.dot(sketch_rows.T, sketch_rows, precision=lax.Precision.HIGHEST)]
    another operation x5 -> x0, matrix products: 2.09 us -> none  [the longest x3 1.61 us: per_device(): jax.scipy.linalg.solve_triangular(chol_factor, sketch_y.T, lower=True)]
    unnamed x0 -> x4, local copies, waits for them, and re-layouts: none -> 1.97 us
where the time goes in v3:
time: 92.8 us; the launch traced here: 92.6 us
  Pallas kernels  90.6 us (98%)
  local copies, waits for them, and re-layouts  1.97 us (2%)
    pallas_call x1, Pallas kernels, keys_and_sketch(): pl.pallas_call(functools.partial(keys_kernel, n), out_shape=(jax.ShapeDty...  70.3 us
    pallas_call x1, Pallas kernels, factor_of(): pl.pallas_call(factor_kernel, out_shape=jax.ShapeDtypeStruct((hidden, ran...  20.3 us
    unnamed x4, local copies, waits for them, and re-layouts  1.97 us

profile of v3, /device:TPU:1, one launch (start us, length us, event | category | flops | bytes accessed | tf_op | source)
XLA Modules:
  0.0 92.6 jit_solution(16817186700873057623)
XLA Ops:
  0.0 70.3 %shard_map.46 = (bf16[924,256]{1,0:T(8,128)(2,1)}, f32[256,256]{1,0:T(8,128)}) custom-call(bf16[16,8192]{1,0:T(8,128)(2,1)} %tok_hbm.1, bf16[924,8192]{1,0:T(8,128)(2,1)} %bitcast.2, bf16[924,8192]{1,0:T(8,128)(2,1)} %bitcast.3, bf16[924,256]{1,0:T(8,128)(2,1)} %test_ref.1), custom_call_target="tpu_custom_call" | custom-call | tf_op jit(solution)/shard_map/pallas_call | solution.py:208
  70.3 0.0 copy-start
  70.3 1.0 %copy-done = bf16[924,256]{1,0:T(8,128)(2,1)S(1)} copy-done((bf16[924,256]{1,0:T(8,128)(2,1)S(1)}, bf16[924,256]{1,0:T(8,128)(2,1)}, u32[]{:S(2)}) %copy-start) | copy-done | bytes 473112
  71.4 0.0 copy-start.1
  71.4 0.9 %copy-done.1 = f32[256,256]{1,0:T(8,128)S(1)} copy-done((f32[256,256]{1,0:T(8,128)S(1)}, f32[256,256]{1,0:T(8,128)}, u32[]{:S(2)}) %copy-start.1) | copy-done | bytes 262168
  72.3 20.3 %shard_map.47 = f32[924,256]{1,0:T(8,128)} custom-call(bf16[924,256]{1,0:T(8,128)(2,1)S(1)} %copy-done, f32[256,256]{1,0:T(8,128)S(1)} %copy-done.1), custom_call_target="tpu_custom_call" | custom-call | tf_op jit(solution)/shard_map/pallas_call | solution.py:302
Async XLA Ops:
  70.3 1.0 %copy-start = (bf16[924,256]{1,0:T(8,128)(2,1)S(1)}, bf16[924,256]{1,0:T(8,128)(2,1)}, u32[]{:S(2)}) copy-start(bf16[924,256]{1,0:T(8,128)(2,1)} %get-tuple-element.7.key_ref) | copy-start | bytes 1419268
  71.4 0.9 %copy-start.1 = (f32[256,256]{1,0:T(8,128)S(1)}, f32[256,256]{1,0:T(8,128)}, u32[]{:S(2)}) copy-start(f32[256,256]{1,0:T(8,128)} %get-tuple-element.8.sketch_ref) | copy-start | bytes 786436

commit v4 on v3

--- a/solution.py
+++ b/solution.py
@@ -9,6 +9,7 @@
 
 MESH = pl.DeviceIdType.MESH
 CHUNKS = 4
+AHEAD = 1
 
 
 def contract(x, y, x_dim, y_dim, precision=None):
@@ -17,13 +18,13 @@
 
 
 def keys_kernel(n, tok_hbm, gate_hbm, up_hbm, test_ref, key_ref, sketch_ref,
-                tok, gw, uw, gacc, uacc, part, sib_sum, half_sum, slices, full,
+                stage, tok, gw, uw, gacc, uacc, part, sib_sum, half_sum, slices, full,
                 loc_sem, w_sem, xs, xr, zs, zr, ys, yr, ss, sr,
                 r0s, r0r, r1s, r1r, r2s, r2r, r3s, r3r):
     t, width = tok_hbm.shape
     kc = width // (2 * CHUNKS)
     chips, lines = n // 2, n // 4
-    rows = n * t
+    rows, half = n * t, n * t // 2
     me = lax.axis_index("ff")
     core, chip = me % 2, me // 2
     b, a = chip % 2, chip // 2
@@ -32,17 +33,23 @@
     def same_core(other_chip):
         return other_chip * 2 + core
 
-    def line_chip(step, side):
-        return ((a - step + lines) % lines) * 2 + side
-
     def send(src, dst, ssem, rsem, target):
         return pltpu.make_async_remote_copy(
             src_ref=src, dst_ref=dst, send_sem=ssem, recv_sem=rsem,
             device_id={"ff": target}, device_id_type=MESH)
 
-    def own_copy(g):
-        return pltpu.make_async_copy(
-            tok_hbm.at[:, pl.ds(g * kc, kc)], tok.at[g, pl.ds(me * t, t), :], loc_sem.at[g])
+    def chip_rows(place, side):
+        return pl.ds(pl.multiple_of((side * lines + place) * 2 * t, 2 * t), 2 * t)
+
+    own_rows = pl.ds(pl.multiple_of(((b * lines + a) * 2 + core) * t, t), t)
+
+    def own_copy(i):
+        g = core * CHUNKS + i
+        return pltpu.make_async_copy(tok_hbm.at[:, pl.ds(g * kc, kc)], tok.at[g, own_rows, :], loc_sem.at[0, i])
+
+    def stage_copy(i):
+        g = (1 - core) * CHUNKS + i
+        return pltpu.make_async_copy(tok_hbm.at[:, pl.ds(g * kc, kc)], stage.at[i], loc_sem.at[1, i])
 
     def gate_copy(g):
         return pltpu.make_async_copy(gate_hbm.at[:, pl.ds(g * kc, kc)], gw.at[g], w_sem.at[0, g])
@@ -51,9 +58,8 @@
         return pltpu.make_async_copy(up_hbm.at[:, pl.ds(g * kc, kc)], uw.at[g], w_sem.at[1, g])
 
     for i in range(CHUNKS):
-        own_copy((1 - core) * CHUNKS + i).start()
-    for i in range(CHUNKS):
-        own_copy(core * CHUNKS + i).start()
+        stage_copy(i).start()
+        own_copy(i).start()
     for i in range(CHUNKS):
         for h in (core, 1 - core):
             gate_copy(h * CHUNKS + i).start()
@@ -65,39 +71,41 @@
         pl.semaphore_signal(barrier, inc=1, device_id={"ff": same_core((chip + d) % chips)}, device_id_type=MESH)
     pl.semaphore_wait(barrier, chips)
 
-    def chip_rows(c):
-        return pl.ds(pl.multiple_of(c * 2 * t, 2 * t), 2 * t)
-
-    def pair_copy(g):
-        own = tok.at[g, pl.ds(me * t, t), :]
-        return send(own, own, xs.at[g], xr.at[g], sibling)
+    def pair_copy(i):
+        return send(stage.at[i], tok.at[(1 - core) * CHUNKS + i, own_rows, :], xs.at[i], xr.at[i], sibling)
 
     def z_copy(i, d):
-        block = tok.at[core * CHUNKS + i, chip_rows(chip), :]
+        block = tok.at[core * CHUNKS + i, chip_rows(a, b), :]
         return send(block, block, zs.at[i, d], zr.at[i, d], same_core(((a + d) % lines) * 2 + b))
 
-    def y_copy(i, d):
-        block = tok.at[core * CHUNKS + i, chip_rows(line_chip(d, b)), :]
-        return send(block, block, ys.at[i, d], yr.at[i, d], same_core(a * 2 + (1 - b)))
-
-    def pass_copy(i, d, other):
-        side = 1 - b if other else b
-        block = tok.at[core * CHUNKS + i, chip_rows(line_chip(d, side)), :]
-        return send(block, block, ss.at[i, other, d], sr.at[i, other, d], sibling)
+    def y_copy(i):
+        line = tok.at[core * CHUNKS + i, pl.ds(pl.multiple_of(b * half, half), half), :]
+        return send(line, line, ys.at[i], yr.at[i], same_core(a * 2 + (1 - b)))
+
+    def pass_copy(i):
+        block = tok.at[core * CHUNKS + i]
+        return send(block, block, ss.at[i], sr.at[i], sibling)
+
+    def cross(i):
+        for d in range(1, lines):
+            z_copy(i, d).wait_recv()
+        y_copy(i).start()
+
+        @pl.when(i + AHEAD < CHUNKS)
+        def _():
+            begin(i + AHEAD)
 
     for i in range(CHUNKS):
-        g = (1 - core) * CHUNKS + i
-        own_copy(g).wait()
-        pair_copy(g).start()
-    for i in range(CHUNKS):
-        g = core * CHUNKS + i
-        own_copy(g).wait()
-        pair_copy(g).start()
-    for i in range(CHUNKS):
-        pair_copy(core * CHUNKS + i).wait_recv()
+        stage_copy(i).wait()
+        pair_copy(i).start()
+    def begin(i):
+        own_copy(i).wait()
+        pair_copy(i).wait_recv()
         for d in range(1, lines):
             z_copy(i, d).start()
-        y_copy(i, 0).start()
+
+    for i in range(AHEAD):
+        begin(i)
 
     gacc[...] = jnp.zeros_like(gacc)
     uacc[...] = jnp.zeros_like(uacc)
@@ -110,30 +118,24 @@
         uacc[...] += contract(uw[g], block, 1, 1)
 
     def chunk(i, carry):
-        for d in range(1, lines):
-            z_copy(i, d).wait_recv()
-            y_copy(i, d).start()
-            pass_copy(i, d, 0).start()
-        for d in range(lines):
-            y_copy(i, d).wait_recv()
-            pass_copy(i, d, 1).start()
+        @pl.when(i + 1 < CHUNKS)
+        def _():
+            cross(i + 1)
+
+        y_copy(i).wait_recv()
+        pass_copy(i).start()
 
         def halves(k, carry):
-            h = (core + k) % 2
-
             @pl.when(k == 1)
             def _():
-                pair_copy((1 - core) * CHUNKS + i).wait_recv()
-                for d in range(lines):
-                    if d > 0:
-                        pass_copy(i, d, 0).wait_recv()
-                    pass_copy(i, d, 1).wait_recv()
-
-            multiply(h * CHUNKS + i)
+                pass_copy(i).wait_recv()
+
+            multiply(((core + k) % 2) * CHUNKS + i)
             return carry
 
         return lax.fori_loop(0, 2, halves, carry)
 
+    cross(jnp.int32(0))
     lax.fori_loop(0, CHUNKS, chunk, 0)
 
     gate = gacc[...]
@@ -141,7 +143,6 @@
     key_ref[...] = keys
     part[...] = contract(keys, test_ref[...], 0, 0)
 
-    half = rows // 2
     pair = send(part.at[pl.ds((1 - core) * half, half), :], sib_sum, r0s, r0r, sibling)
     pair.start()
     pair.wait_recv()
@@ -179,13 +180,10 @@
 
     def drain(i, carry):
         pair_copy(i).wait_send()
-        pair_copy(CHUNKS + i).wait_send()
-        for d in range(lines):
-            if d > 0:
-                z_copy(i, d).wait_send()
-                pass_copy(i, d, 0).wait_send()
-            y_copy(i, d).wait_send()
-            pass_copy(i, d, 1).wait_send()
+        for d in range(1, lines):
+            z_copy(i, d).wait_send()
+        y_copy(i).wait_send()
+        pass_copy(i).wait_send()
         return carry
 
     lax.fori_loop(0, CHUNKS, drain, 0)
@@ -211,6 +209,7 @@
         in_specs=[pl.BlockSpec(memory_space=pl.ANY)] * 3 + [pl.BlockSpec(memory_space=pltpu.VMEM)],
         out_specs=(pl.BlockSpec(memory_space=pltpu.VMEM),) * 2,
         scratch_shapes=[
+            vmem((CHUNKS, t, kc), bf16),
             vmem((2 * CHUNKS, rows, kc), bf16),
             vmem((2 * CHUNKS, hidden, kc), bf16),
             vmem((2 * CHUNKS, hidden, kc), bf16),
@@ -221,12 +220,12 @@
             vmem((rows // 2, rank), f32),
             vmem((chips, t, rank), f32),
             vmem((rows, rank), f32),
-            dma((2 * CHUNKS,)),
+            dma((2, CHUNKS)),
             dma((2, 2 * CHUNKS)),
-            dma((2 * CHUNKS,)), dma((2 * CHUNKS,)),
+            dma((CHUNKS,)), dma((CHUNKS,)),
             dma((CHUNKS, lines)), dma((CHUNKS, lines)),
-            dma((CHUNKS, lines)), dma((CHUNKS, lines)),
-            dma((CHUNKS, 2, lines)), dma((CHUNKS, 2, lines)),
+            dma((CHUNKS,)), dma((CHUNKS,)),
+            dma((CHUNKS,)), dma((CHUNKS,)),
             dma, dma,
             dma((chips,)), dma((chips,)),
             dma((chips,)), dma((chips,)),
@@ -237,7 +236,9 @@
     )(tokens, gate_weight, up_weight, test_matrix)
 
 
-def factor_kernel(key_ref, sketch_ref, out_ref, work):
+def factor_kernel(key_hbm, sketch_ref, out_ref, work, key_ref, key_sem):
+    load = pltpu.make_async_copy(key_hbm, key_ref, key_sem)
+    load.start()
     rank = out_ref.shape[1]
     span = work.shape[1]
     tile, step = 128, 8
@@ -292,6 +293,7 @@
     basis = work[:, rank:]
     high = basis.astype(jnp.bfloat16)
     rest = (basis - high.astype(jnp.float32)).astype(jnp.bfloat16)
+    load.wait()
     keys = key_ref[...]
     out_ref[...] = contract(keys, high, 1, 1) + contract(keys, rest, 1, 1)
 
@@ -302,9 +304,13 @@
     return pl.pallas_call(
         factor_kernel,
         out_shape=jax.ShapeDtypeStruct((hidden, rank), jnp.float32),
-        in_specs=[pl.BlockSpec(memory_space=pltpu.VMEM)] * 2,
+        in_specs=[pl.BlockSpec(memory_space=pl.ANY), pl.BlockSpec(memory_space=pltpu.VMEM)],
         out_specs=pl.BlockSpec(memory_space=pltpu.VMEM),
-        scratch_shapes=[pltpu.VMEM((rank, rank + rows), jnp.float32)],
+        scratch_shapes=[
+            pltpu.VMEM((rank, rank + rows), jnp.float32),
+            pltpu.VMEM((hidden, rows), jnp.bfloat16),
+            pltpu.SemaphoreType.DMA,
+        ],
         compiler_params=pltpu.CompilerParams(vmem_limit_bytes=32 * 2**20),
     )(key_rows, sketch_rows)
 

time: 92.8 us -> 84 us (0.905)
  Pallas kernels: 90.6 us -> 81.8 us
    pallas_call x1, Pallas kernels: 70.3 us -> 61.2 us  [keys_and_sketch(): pl.pallas_call(functools.partial(keys_kernel, n), out_shape=(jax.ShapeDty...]
where the time goes in v4:
time: 84 us; the launch traced here: 83.8 us
  Pallas kernels  81.8 us (97%)
  local copies, waits for them, and re-layouts  1.97 us (2%)
    pallas_call x1, Pallas kernels, keys_and_sketch(): pl.pallas_call(functools.partial(keys_kernel, n), out_shape=(jax.ShapeDty...  61.2 us
    pallas_call x1, Pallas kernels, factor_of(): pl.pallas_call(factor_kernel, out_shape=jax.ShapeDtypeStruct((hidden, ran...  20.6 us
    unnamed x4, local copies, waits for them, and re-layouts  1.97 us

profile of v4, /device:TPU:1, one launch (start us, length us, event | category | flops | bytes accessed | tf_op | source)
XLA Modules:
  0.0 83.8 jit_solution(5383154011423385242)
XLA Ops:
  0.0 61.2 %shard_map.46 = (bf16[924,256]{1,0:T(8,128)(2,1)}, f32[256,256]{1,0:T(8,128)}) custom-call(bf16[16,8192]{1,0:T(8,128)(2,1)} %tok_hbm.1, bf16[924,8192]{1,0:T(8,128)(2,1)} %bitcast.2, bf16[924,8192]{1,0:T(8,128)(2,1)} %bitcast.3, bf16[924,256]{1,0:T(8,128)(2,1)} %test_ref.1), custom_call_target="tpu_custom_call" | custom-call | tf_op jit(solution)/shard_map/pallas_call | solution.py:206
  61.2 0.0 copy-start
  61.2 1.0 %copy-done = bf16[924,256]{1,0:T(8,128)(2,1)S(1)} copy-done((bf16[924,256]{1,0:T(8,128)(2,1)S(1)}, bf16[924,256]{1,0:T(8,128)(2,1)}, u32[]{:S(2)}) %copy-start) | copy-done | bytes 473112
  62.2 0.0 copy-start.1
  62.2 0.9 %copy-done.1 = f32[256,256]{1,0:T(8,128)S(1)} copy-done((f32[256,256]{1,0:T(8,128)S(1)}, f32[256,256]{1,0:T(8,128)}, u32[]{:S(2)}) %copy-start.1) | copy-done | bytes 262168
  63.2 20.6 %shard_map.47 = f32[924,256]{1,0:T(8,128)} custom-call(bf16[924,256]{1,0:T(8,128)(2,1)S(1)} %copy-done, f32[256,256]{1,0:T(8,128)S(1)} %copy-done.1), custom_call_target="tpu_custom_call" | custom-call | tf_op jit(solution)/shard_map/pallas_call | solution.py:304
Async XLA Ops:
  61.2 1.0 %copy-start = (bf16[924,256]{1,0:T(8,128)(2,1)S(1)}, bf16[924,256]{1,0:T(8,128)(2,1)}, u32[]{:S(2)}) copy-start(bf16[924,256]{1,0:T(8,128)(2,1)} %get-tuple-element.7.key_hbm) | copy-start | bytes 1419268
  62.2 0.9 %copy-start.1 = (f32[256,256]{1,0:T(8,128)S(1)}, f32[256,256]{1,0:T(8,128)}, u32[]{:S(2)}) copy-start(f32[256,256]{1,0:T(8,128)} %get-tuple-element.8.sketch_ref) | copy-start | bytes 786436
